TPU v7x, 32 devices: a whole 2x2x4 slice. The times are simulated.
32 devices in a mesh: groups: 2 (over x), row: 4 (over z), col: 4 (over y, core).
Axes of the slice: x: 2, y: 2, z: 4, core: 2. Of those that a mesh axis runs over, the one named last changes fastest.
Arguments:
- pair: bfloat16 [288, 144, 128], P(('groups', 'row'), 'col'), parts along dimension 0, may hold values from -6 to 6
- token_mask: int32 [288], P('groups'), parts along dimension 0, may hold values 0 or 1
- in_gain: float32 [128], replicated, may hold values from 0.1 to 1.9
- in_bias: float32 [128], replicated, may hold values from -3 to 3
- w_in: bfloat16 [128, 512], replicated, may hold values from -0.5 to 0.5
- w_gate: bfloat16 [128, 128], replicated, may hold values from -0.5 to 0.5
- out_gain: float32 [128], replicated, may hold values from 0.1 to 1.9
- out_bias: float32 [128], replicated, may hold values from -3 to 3
- w_out: bfloat16 [128, 128], replicated, may hold values from -0.5 to 0.5
Outputs:
- update: bfloat16 [288, 144, 128], P(('groups', 'row'), 'col'), parts along dimension 0
There are 2 independent parts, one for each index of `groups`. A program takes and returns all parts, laid end to end along the dimension named above; an argument that names none is the same for every part. Nothing has to cross between parts.
Inputs may be any that keep to these rules, and one draw needn't show every extreme that they name: `token_mask`: one 0/1 residue flag per token.
All inputs are finite; a program needn't handle non-finite values.
Results may differ from a plain program's by a relative error of at most 0.0052.
Values may be sent and summed in bfloat16 or wider, within the bound.
A program may use at most 128 MiB of HBM per device.

v0:
```python
import jax
import jax.numpy as jnp
from jax import lax
from jax.sharding import PartitionSpec as P


def layer_norm(values, gain, bias):
    average = jnp.mean(values, axis=-1, keepdims=True)
    centred = values - average
    variance = jnp.mean(centred * centred, axis=-1, keepdims=True)
    return centred * lax.rsqrt(variance + 1e-05) * gain + bias


def local(pair, token_mask, in_gain, in_bias, w_in, w_gate, out_gain, out_bias, w_out):
    row_tok, col_tok, channels = pair.shape
    hidden = w_out.shape[0]
    col_index = lax.axis_index("col")
    row_start = lax.axis_index("row") * row_tok
    col_start = col_index * col_tok
    row_flags = lax.dynamic_slice_in_dim(token_mask, row_start, row_tok, 0).astype(jnp.float32)
    col_flags = lax.dynamic_slice_in_dim(token_mask, col_start, col_tok, 0).astype(jnp.float32)
    normed = layer_norm(pair.astype(jnp.float32), in_gain, in_bias).astype(jnp.bfloat16)
    flat = normed.reshape(row_tok * col_tok, channels)
    proj = jnp.dot(flat, w_in, preferred_element_type=jnp.float32).reshape(
        row_tok, col_tok, 4, hidden
    )
    pmask = (row_flags[:, None] * col_flags[None, :])[:, :, None]
    left = (jax.nn.sigmoid(proj[:, :, 0]) * proj[:, :, 1] * pmask).astype(jnp.bfloat16)
    right = (jax.nn.sigmoid(proj[:, :, 2]) * proj[:, :, 3] * pmask).astype(jnp.bfloat16)
    right_all = lax.all_gather(right, "row", axis=0, tiled=True)
    right_own = lax.all_to_all(right_all, "col", split_axis=0, concat_axis=1, tiled=True)
    triangle = jnp.einsum(
        "ikh,jkh->ijh",
        lax.all_gather(left, "col", axis=1, tiled=True),
        right_own,
        preferred_element_type=jnp.float32,
    )
    tnorm = layer_norm(triangle, out_gain, out_bias).astype(jnp.bfloat16)
    gating = jax.nn.sigmoid(jnp.dot(flat, w_gate, preferred_element_type=jnp.float32))
    projected = jnp.dot(
        tnorm.reshape(row_tok * col_tok, hidden), w_out, preferred_element_type=jnp.float32
    )
    return (gating * projected).reshape(row_tok, col_tok, channels).astype(jnp.bfloat16)


def solution(mesh):
    placed = (P(("groups", "row"), "col", None), P("groups"), P(), P(), P(), P(), P(), P(), P())
    return jax.shard_map(
        local,
        mesh=mesh,
        in_specs=placed,
        out_specs=P(("groups", "row"), "col", None),
        check_vma=False,
    )
```

profile of v0, /device:TPU:0, one launch (start us, length us, event | category | flops | bytes accessed | tf_op | source)
XLA Modules:
  0.0 103.7 jit_solution(16243388103681451536)
XLA Ops:
  6.5 1.3 %convert_reduce_fusion = f32[36,36]{1,0:T(8,128)S(1)} fusion(bf16[36,36,128]{2,1,0:T(8,128)(2,1)} %param.9), kind=kLoop, calls=%fused_computation.9 | loop fusion | flops 330480 | bytes 336960 | tf_op jit(solution)/shard_map/reduce_sum | solution.py:8
  7.8 1.5 %fusion.6 = f32[36,36]{1,0:T(8,128)S(1)} fusion(bf16[36,36,128]{2,1,0:T(8,128)(2,1)} %param.9, f32[36,36]{1,0:T(8,128)S(1)} %broadcast_multiply_fusion.2), kind=kLoop, calls=%fused_computation.12 | loop fusion | flops 662256 | bytes 342144 | tf_op jit(solution)/shard_map/reduce_sum | solution.py:10
  9.3 1.0 copy.71
  10.3 0.8 dynamic-slice_convert_fusion.1
  11.2 0.1 broadcast_multiply_fusion
  11.2 1.5 %fusion.9 = bf16[36,36,128]{2,1,0:T(8,128)(2,1)S(1)} fusion(bf16[36,36,128]{2,1,0:T(8,128)(2,1)} %param.9, f32[128]{0:T(128)} %param.12, f32[128]{0:T(128)} %param.11, f32[36,36]{1,0:T(8,128)S(1)} %add_rsqrt_fusion.1, f32[36,36]{1,0:T(8,128)S(1)} %broadcast_multiply_fusion.2), kind=kLoop, calls=%fused_computation.15 | loop fusion | flops 995328 | bytes 674944 | tf_op jit(solution)/shard_map/convert_element_type | solution.py:22
  12.7 0.6 fusion.26
  13.3 1.2 %fusion.12 = (bf16[36,36,128]{2,1,0:T(8,128)(2,1)S(1)}, bf16[36,36,128]{2,1,0:T(8,128)(2,1)}) fusion(f32[36,36,4,128]{3,1,2,0:T(8,128)S(1)} %fusion.26, f32[36,36]{1,0:T(8,128)S(1)} %broadcast_multiply_fusion), kind=kLoop, calls=%fused_computation.19 | loop fusion | flops 1990656 | bytes 3322944 | tf_op jit(solution)/shard_map/convert_element_type | solution.py:28
  14.5 0.8 copy.62
  15.4 37.5 %all-gather.3.cloned.1.call-done = bf16[144,36,128]{2,1,0:T(8,128)(2,1)} async-done(((bf16[36,36,128]{2,1,0:T(8,128)(2,1)}), bf16[144,36,128]{2,1,0:T(8,128)(2,1)}) %all-gather.3.cloned.1.call-update) | async-done | bytes 1327120 | tf_op jit(solution)/shard_map/all_gather | solution.py:30
  52.8 3.6 %all-to-all-start = ((bf16[144,36,128]{2,1,0:T(8,128)(2,1)}), bf16[144,36,128]{2,1,0:T(8,128)(2,1)S(1)}, u32[]{:S(2)}, u32[]{:S(2)}) async-start(bf16[144,36,128]{2,1,0:T(8,128)(2,1)} %all-gather.3.cloned.1.call-done), calls=%async_computation | async-start | bytes 2949120 | tf_op jit(solution)/shard_map/all_to_all | solution.py:31
  56.5 1.2 %fusion.2 = f32[1296,128]{1,0:T(8,128)} fusion(bf16[1296,128]{1,0:T(8,128)(2,1)S(1)} %reshape.79, bf16[128,128]{1,0:T(8,128)(2,1)S(1)} %copy-done), kind=kOutput, calls=%fused_computation.5 | convolution fusion | flops 42964992 | bytes 1028096 | tf_op jit(solution)/shard_map/dot_general | solution.py:39
  57.7 22.8 %all-gather.5.cloned.1.call-done = bf16[36,144,128]{2,0,1:T(8,128)(2,1)} async-done(((bf16[36,36,128]{2,0,1:T(8,128)(2,1)}), bf16[36,144,128]{2,0,1:T(8,128)(2,1)}) %all-gather.5.cloned.1.call-update) | async-done | bytes 1327120 | tf_op jit(solution)/shard_map/all_gather | solution.py:34
  80.4 5.3 %copy.64 = bf16[36,144,128]{1,0,2:T(8,128)(2,1)} copy(bf16[36,144,128]{2,0,1:T(8,128)(2,1)} %all-gather.5.cloned.1.call-done) | data formatting | bytes 2654208 | tf_op jit(solution)/shard_map/all_gather | solution.py:34
  85.7 0.3 copy.78
  85.9 0.3 all_to_all.16
  86.2 3.6 %copy.63 = bf16[36,144,128]{1,0,2:T(8,128)(2,1)} copy(bf16[36,144,128]{2,1,0:T(8,128)(2,1)S(1)} %all_to_all.16) | data formatting | bytes 2654208 | tf_op jit(solution)/shard_map/all_to_all | solution.py:31
  89.8 3.4 %bitcast_reduce_fusion = (f32[36,36]{0,1:T(8,128)S(1)}, f32[128,36,36]{2,1,0:T(8,128)S(1)}) fusion(bf16[36,144,128]{1,0,2:T(8,128)(2,1)} %copy.63, bf16[36,144,128]{1,0,2:T(8,128)(2,1)} %copy.64), kind=kOutput, calls=%fused_computation | convolution fusion | flops 47940336 | bytes 3322944 | tf_op jit(solution)/shard_map/ikh,jkh->ijh/dot_general | solution.py:32
  93.2 1.3 %copy.65 = f32[128,36,36]{0,1,2:T(8,128)S(1)} copy(f32[128,36,36]{2,1,0:T(8,128)S(1)} %get-tuple-element.10) | data formatting | bytes 1327104 | tf_op jit(solution)/shard_map/ikh,jkh->ijh/dot_general | solution.py:32
  94.5 0.1 copy.67
  94.6 0.5 multiply_reduce_fusion
  95.1 0.5 add_convert_fusion
  95.7 0.3 fusion.3
  96.0 0.8 convert_element_type.35
  (21 shorter events, 0.3 us)
Async XLA Ops:
  6.5 49.9 %copy-start = (bf16[128,128]{1,0:T(8,128)(2,1)S(1)}, bf16[128,128]{1,0:T(8,128)(2,1)}, u32[]{:S(2)}) copy-start(bf16[128,128]{1,0:T(8,128)(2,1)} %param.14) | copy-start | bytes 98308
  6.5 46.3 %all-gather.3.cloned.1.call-start = ((), (), s32[]{:S(2)}) async-start(), calls=%async_computation.1 | async-start | bytes 1843200 | tf_op jit(solution)/shard_map/all_gather | solution.py:30
  14.5 65.9 %all-gather.5.cloned.1.call-start = ((), (), s32[]{:S(2)}) async-start(), calls=%async_computation.2 | async-start | bytes 1843200 | tf_op jit(solution)/shard_map/all_gather | solution.py:34
  52.8 32.9 %all-to-all-start = ((bf16[144,36,128]{2,1,0:T(8,128)(2,1)}), bf16[144,36,128]{2,1,0:T(8,128)(2,1)S(1)}, u32[]{:S(2)}, u32[]{:S(2)}) async-start(bf16[144,36,128]{2,1,0:T(8,128)(2,1)} %all-gather.3.cloned.1.call-done), calls=%async_computation | async-start | bytes 2949120 | tf_op jit(solution)/shard_map/all_to_all | solution.py:31
  93.2 1.9 %copy-start.3 = (f32[128]{0:T(128)S(1)}, f32[128]{0:T(128)}, u32[]{:S(2)}) copy-start(f32[128]{0:T(128)} %param.16) | copy-start | bytes 1540
  93.2 1.9 %copy-start.4 = (f32[128]{0:T(128)S(1)}, f32[128]{0:T(128)}, u32[]{:S(2)}) copy-start(f32[128]{0:T(128)} %param.15) | copy-start | bytes 1540
  93.2 2.5 %copy-start.2 = (bf16[128,128]{1,0:T(8,128)(2,1)S(1)}, bf16[128,128]{1,0:T(8,128)(2,1)}, u32[]{:S(2)}) copy-start(bf16[128,128]{1,0:T(8,128)(2,1)} %param.17) | copy-start | bytes 98308
  94.5 1.2 %copy-start.1 = (f32[1296,128]{1,0:T(8,128)S(1)}, f32[1296,128]{1,0:T(8,128)}, u32[]{:S(2)}) copy-start(f32[1296,128]{1,0:T(8,128)} %fusion.2) | copy-start | bytes 1990660
Sparse Core Ops, SparseCore 0:
  14.6 38.1 all-gather.2
  54.4 25.9 all-gather.4
where the time goes:
time: 104 us
  waiting for transfers between devices  60.3 us (58%)
  between operations  13.6 us (13%)
  local copies, waits for them, and re-layouts  13.5 us (13%)
  other arithmetic  7.22 us (7%)
  matrix products  5.44 us (5%)
  starting transfers between devices  3.6 us (3%)
    all_gather x1, waiting for transfers between devices, local(): right_all = lax.all_gather(right, 'row', axis=0, tiled=True)  37.5 us
    all_gather x1, waiting for transfers between devices, local(): lax.all_gather(left, 'col', axis=1, tiled=True)  22.8 us
    all_gather x1, local copies, waits for them, and re-layouts, local(): lax.all_gather(left, 'col', axis=1, tiled=True)  5.25 us
    all_to_all x3, local copies, waits for them, and re-layouts, local(): lax.all_to_all(right_all, 'col', split_axis=0, concat_axis=1, tiled=True)  4.14 us
    all_to_all x1, starting transfers between devices, local(): lax.all_to_all(right_all, 'col', split_axis=0, concat_axis=1, tiled=True)  3.55 us
    dot_general x1, matrix products, local(): jnp.einsum('ikh,jkh->ijh', lax.all_gather(left, 'col', axis=1, tiled=True...  3.36 us
  transfers between devices with their start and end apart: 3, of which 2 were waited for; matrix products, arithmetic and copies ran while one was open for 7% of the time, Pallas kernels for 0%

commit v1 on v0

v1 whole, which is shorter than its diff:
```python
import functools

import jax
import jax.numpy as jnp
from jax import lax
from jax.experimental import pallas as pl
from jax.experimental.pallas import tpu as pltpu
from jax.sharding import PartitionSpec as P

MESH = pl.DeviceIdType.MESH
JTILE = 4


def sigmoid(values):
    return 0.5 * jnp.tanh(0.5 * values) + 0.5


def layer_norm(values, gain, bias):
    average = jnp.mean(values, axis=-1, keepdims=True)
    centred = values - average
    variance = jnp.mean(centred * centred, axis=-1, keepdims=True)
    return centred * lax.rsqrt(variance + 1e-05) * gain + bias


def kernel(
    nrow, ncol, row_tok, col_tok, parts,
    pair_ref, pair_t_ref, mask_ref, mask_t_ref, in_gain, in_bias, w_in, w_gate, out_gain, out_bias, w_out,
    out_ref,
    blocks, left, gate, wide, stage, sums_out, sums_own, sums_in,
    z_send, z_recv, p_send, p_recv,
):
    hidden = w_out.shape[0]
    group, row, col = lax.axis_index("groups"), lax.axis_index("row"), lax.axis_index("col")
    per_row = row_tok // col_tok
    chunks = per_row * parts
    chunk_j = col_tok // parts
    rows = chunk_j * col_tok
    sum_rows = chunk_j * row_tok
    has_up, has_down = row < nrow - 1, row > 0

    barrier = pltpu.get_barrier_semaphore()

    @pl.when(has_up)
    def _():
        pl.semaphore_signal(barrier, inc=1, device_id=(group, row + 1, col), device_id_type=MESH)

    @pl.when(has_down)
    def _():
        pl.semaphore_signal(barrier, inc=1, device_id=(group, row - 1, col), device_id_type=MESH)

    for step in range(1, ncol):
        peer = lax.rem(col + step, ncol)
        pl.semaphore_signal(barrier, inc=1, device_id=(group, row, peer), device_id_type=MESH)

    def up_copy(block, chunk):
        at = blocks.at[block, chunk]
        return pltpu.make_async_remote_copy(
            at, at, z_send.at[0, block, chunk], z_recv.at[block, chunk], (group, row + 1, col), MESH
        )

    def down_copy(block, chunk):
        at = blocks.at[block, chunk]
        return pltpu.make_async_remote_copy(
            at, at, z_send.at[1, block, chunk], z_recv.at[block, chunk], (group, row - 1, col), MESH
        )

    def sum_copy(target, source, part):
        return pltpu.make_async_remote_copy(
            sums_out.at[target, part], sums_in.at[source, part],
            p_send.at[target, part], p_recv.at[source, part], (group, row, target), MESH,
        )

    gain, bias = in_gain[...], in_bias[...]

    for chunk in range(chunks):
        span = pl.ds(chunk * rows, rows)
        normed = layer_norm(pair_ref[span, :].astype(jnp.float32), gain, bias).astype(jnp.bfloat16)
        proj = jnp.dot(normed, w_in[:, 2 * hidden :], preferred_element_type=jnp.float32)
        right = sigmoid(proj[:, :hidden]) * proj[:, hidden:] * mask_ref[span, :]
        blocks[row, chunk] = right.astype(jnp.bfloat16)
        if chunk == 0:
            neighbours = has_up.astype(jnp.int32) + has_down.astype(jnp.int32)
            pl.semaphore_wait(barrier, ncol - 1 + neighbours)

        @pl.when(has_up)
        def _():
            up_copy(row, chunk).start()

        @pl.when(has_down)
        def _():
            down_copy(row, chunk).start()

    k_step = col_tok // parts
    for part in range(parts):
        span = pl.ds(part * sum_rows, sum_rows)
        normed = layer_norm(pair_t_ref[span, :].astype(jnp.float32), gain, bias).astype(jnp.bfloat16)
        proj = jnp.dot(normed, w_in[:, : 2 * hidden], preferred_element_type=jnp.float32)
        value = sigmoid(proj[:, :hidden]) * proj[:, hidden:] * mask_t_ref[span, :]
        value = value.astype(jnp.bfloat16).astype(jnp.float32)
        for k in range(k_step):
            left[part * k_step + k, :row_tok, :] = value[k * row_tok : (k + 1) * row_tok]
        gate[span, :] = sigmoid(jnp.dot(normed, w_gate[...], preferred_element_type=jnp.float32))

    def partial_sums(block, chunk):
        target, part = block * per_row + chunk // parts, lax.rem(chunk, parts)
        wide[...] = blocks[block, chunk].astype(jnp.float32)

        def tile(at, carry):
            start = pl.multiple_of(at * (JTILE * col_tok), 16)
            totals = [jnp.zeros((row_tok, hidden), jnp.float32) for _ in range(JTILE)]
            for k in range(col_tok):
                lines = left[k, :row_tok, :]
                for j in range(JTILE):
                    totals[j] += wide[pl.ds(start + (j * col_tok + k), 1), :] * lines
            for j in range(JTILE):
                stage[j * row_tok : (j + 1) * row_tok, :] = totals[j]
            span = pl.ds(pl.multiple_of(at * (JTILE * row_tok), 16), JTILE * row_tok)

            @pl.when(target == col)
            def _():
                sums_own[part, span, :] = stage[...]

            @pl.when(target != col)
            def _():
                sums_out[target, part, span, :] = stage[...].astype(jnp.bfloat16)

            return carry

        lax.fori_loop(0, chunk_j // JTILE, tile, 0)

        @pl.when(target != col)
        def _():
            sum_copy(target, col, part).start()

    def own_step(chunk, carry):
        partial_sums(row, chunk)
        return carry

    lax.fori_loop(0, chunks, own_step, 0)

    def arrival(index, carry):
        step = index // (2 * chunks) + 1
        within = lax.rem(index, 2 * chunks)
        chunk, above = within // 2, lax.rem(within, 2)
        block = row - step + above * (2 * step)

        @pl.when((block >= 0) & (block < nrow))
        def _():
            @pl.when(above == 0)
            def _():
                down_copy(block, chunk).wait_recv()

                @pl.when(has_up)
                def _():
                    up_copy(block, chunk).start()

            @pl.when(above == 1)
            def _():
                up_copy(block, chunk).wait_recv()

                @pl.when(has_down)
                def _():
                    down_copy(block, chunk).start()

            partial_sums(block, chunk)

        return carry

    lax.fori_loop(0, 2 * chunks * (nrow - 1), arrival, 0)

    for part in range(parts):
        total = sums_own[part]
        for step in range(1, ncol):
            source = lax.rem(col + step, ncol)
            sum_copy(source, source, part).wait_recv()
            total += sums_in[source, part].astype(jnp.float32)
        normed = layer_norm(total, out_gain[...], out_bias[...]).astype(jnp.bfloat16)
        projected = jnp.dot(normed, w_out[...], preferred_element_type=jnp.float32)
        span = pl.ds(part * sum_rows, sum_rows)
        out_ref[span, :] = (gate[span, :] * projected).astype(jnp.bfloat16)

    def drain_rows(index, carry):
        block, chunk = index // chunks, lax.rem(index, chunks)

        @pl.when(has_up & (block <= row))
        def _():
            up_copy(block, chunk).wait_send()

        @pl.when(has_down & (block >= row))
        def _():
            down_copy(block, chunk).wait_send()

        return carry

    lax.fori_loop(0, nrow * chunks, drain_rows, 0)
    for step in range(1, ncol):
        target = lax.rem(col + step, ncol)
        for part in range(parts):
            sum_copy(target, col, part).wait_send()


def local(nrow, ncol, pair, token_mask, in_gain, in_bias, w_in, w_gate, out_gain, out_bias, w_out):
    row_tok, col_tok, channels = pair.shape
    hidden = w_out.shape[0]
    parts = 3
    row_start = lax.axis_index("row") * row_tok
    col_start = lax.axis_index("col") * col_tok
    row_flags = lax.dynamic_slice_in_dim(token_mask, row_start, row_tok, 0).astype(jnp.float32)
    col_flags = lax.dynamic_slice_in_dim(token_mask, col_start, col_tok, 0).astype(jnp.float32)
    total = row_tok * col_tok
    mask = (row_flags[:, None] * col_flags[None, :]).reshape(total, 1)
    mask_t = (col_flags[:, None] * row_flags[None, :]).reshape(total, 1)
    chunks = row_tok // col_tok * parts
    rows = col_tok // parts * col_tok
    sum_rows = col_tok // parts * row_tok
    padded = -(-row_tok // 8) * 8
    vmem = pl.BlockSpec(memory_space=pltpu.VMEM)
    result = pl.pallas_call(
        functools.partial(kernel, nrow, ncol, row_tok, col_tok, parts),
        out_shape=jax.ShapeDtypeStruct((total, channels), jnp.bfloat16),
        in_specs=[vmem] * 11,
        out_specs=vmem,
        scratch_shapes=[
            pltpu.VMEM((nrow, chunks, rows, hidden), jnp.bfloat16),
            pltpu.VMEM((col_tok, padded, hidden), jnp.float32),
            pltpu.VMEM((total, channels), jnp.float32),
            pltpu.VMEM((rows, hidden), jnp.float32),
            pltpu.VMEM((JTILE * row_tok, hidden), jnp.float32),
            pltpu.VMEM((ncol, parts, sum_rows, hidden), jnp.bfloat16),
            pltpu.VMEM((parts, sum_rows, hidden), jnp.float32),
            pltpu.VMEM((ncol, parts, sum_rows, hidden), jnp.bfloat16),
            pltpu.SemaphoreType.DMA((2, nrow, chunks)),
            pltpu.SemaphoreType.DMA((nrow, chunks)),
            pltpu.SemaphoreType.DMA((ncol, parts)),
            pltpu.SemaphoreType.DMA((ncol, parts)),
        ],
        compiler_params=pltpu.CompilerParams(
            collective_id=0, has_side_effects=True, vmem_limit_bytes=56 * 1024 * 1024
        ),
    )(
        pair.reshape(total, channels),
        pair.transpose(1, 0, 2).reshape(total, channels),
        mask,
        mask_t,
        in_gain[None, :],
        in_bias[None, :],
        w_in,
        w_gate,
        out_gain[None, :],
        out_bias[None, :],
        w_out,
    )
    return result.reshape(col_tok, row_tok, channels).transpose(1, 0, 2)


def solution(mesh):
    placed = (P(("groups", "row"), "col", None), P("groups"), P(), P(), P(), P(), P(), P(), P())
    return jax.shard_map(
        functools.partial(local, mesh.shape["row"], mesh.shape["col"]),
        mesh=mesh,
        in_specs=placed,
        out_specs=P(("groups", "row"), "col", None),
        check_vma=False,
    )
```

time: 104 us -> 41.3 us (0.40)
  waiting for transfers between devices: 60.3 us -> 0 us
  Pallas kernels: 0 us -> 33.3 us
  between operations: 13.6 us -> 0.02 us
  other arithmetic: 7.22 us -> 0.15 us
  local copies, waits for them, and re-layouts: 13.5 us -> 7.35 us
  matrix products: 5.44 us -> 0 us
  starting transfers between devices: 3.6 us -> 0 us
    all_gather x2 -> x0, waiting for transfers between devices: 60.2 us -> none  [the longest x1 37.5 us: local(): right_all = lax.all_gather(right, 'row', axis=0, tiled=True)]
    pallas_call x0 -> x1, Pallas kernels: none -> 33.3 us  [local(): pl.pallas_call(functools.partial(kernel, nrow, ncol, row_tok, col_tok, pa...]
    dot_general x4 -> x0, matrix products: 5.44 us -> none  [the longest x1 3.36 us: local(): jnp.einsum('ikh,jkh->ijh', lax.all_gather(left, 'col', axis=1, tiled=True...]
    all_gather x1 -> x0, local copies, waits for them, and re-layouts: 5.25 us -> none  [local(): lax.all_gather(left, 'col', axis=1, tiled=True)]
    reshape x2 -> x4, local copies, waits for them, and re-layouts: 0.13 us -> 4.44 us  [the longest x2 1.83 us: local(): return result.reshape(col_tok, row_tok, channels).transpose(1, 0, 2)]
    all_to_all x3 -> x0, local copies, waits for them, and re-layouts: 4.14 us -> none  [local(): lax.all_to_all(right_all, 'col', split_axis=0, concat_axis=1, tiled=True)]
    all_to_all x1 -> x0, starting transfers between devices: 3.55 us -> none  [local(): lax.all_to_all(right_all, 'col', split_axis=0, concat_axis=1, tiled=True)]
    reduce_sum x3 -> x0, other arithmetic: 3.21 us -> none  [the longest x2 1.95 us: layer_norm(): variance = jnp.mean(centred * centred, axis=-1, keepdims=True)]
  transfers between devices with their start and end apart: 3 -> 0, of which waited for: 2 -> 0; matrix products, arithmetic and copies ran while one was open for 7% -> 0% of each run, Pallas kernels for 0% -> 0%
where the time goes in v1:
time: 41.3 us; the launch traced here: 40.8 us
  Pallas kernels  33.3 us (81%)
  local copies, waits for them, and re-layouts  7.35 us (18%)
    pallas_call x1, Pallas kernels, local(): pl.pallas_call(functools.partial(kernel, nrow, ncol, row_tok, col_tok, pa...  33.3 us
    reshape x2, local copies, waits for them, and re-layouts, local(): return result.reshape(col_tok, row_tok, channels).transpose(1, 0, 2)  1.83 us
    reshape x1, local copies, waits for them, and re-layouts, local(): pair.reshape(total, channels)  1.82 us
    mul x1, local copies, waits for them, and re-layouts, local(): mask = (row_flags[:, None] * col_flags[None, :]).reshape(total, 1)  1.09 us
    mul x1, local copies, waits for them, and re-layouts, local(): mask_t = (col_flags[:, None] * row_flags[None, :]).reshape(total, 1)  1.09 us

profile of v1, /device:TPU:0, one launch (start us, length us, event | category | flops | bytes accessed | tf_op | source)
XLA Modules:
  0.0 40.8 jit_solution(11528392953958322180)
XLA Ops:
  0.0 0.0 copy-start.1
  0.0 0.7 %copy-done.1 = s32[144]{0:T(256)S(1)} copy-done((s32[144]{0:T(256)S(1)}, s32[144]{0:T(256)}, u32[]{:S(2)}) %copy-start.1) | copy-done | bytes 600
  0.7 0.1 dynamic-slice_convert_fusion.1
  0.8 0.0 copy-start
  0.8 0.1 broadcast_multiply_fusion
  0.8 1.8 %reshape.59.pair_ref = bf16[1296,128]{1,0:T(8,128)(2,1)} reshape(bf16[36,36,128]{2,1,0:T(8,128)(2,1)} %param.9) | data formatting | bytes 663552 | tf_op jit(solution)/shard_map/reshape | solution.py:241
  2.7 0.0 copy-done
  2.7 0.1 copy.12
  2.7 0.8 %reshape.60.pair_t_ref = bf16[1296,128]{1,0:T(8,128)(2,1)} reshape(bf16[36,36,128]{2,1,0:T(8,128)(2,1)S(1)} %copy.12) | data formatting | bytes 663552 | tf_op jit(solution)/shard_map/reshape | solution.py:242
  3.5 1.1 %mul.63.mask_t_ref = f32[1296,1]{1,0:T(8,128)} reshape(f32[36,36]{1,0:T(8,128)S(1)} %get-tuple-element.5) | data formatting | bytes 10368 | tf_op jit(solution)/shard_map/mul | solution.py:212
  4.6 1.1 %mul.62.mask_ref = f32[1296,1]{1,0:T(8,128)} reshape(f32[36,36]{1,0:T(8,128)S(1)} %get-tuple-element.6) | data formatting | bytes 10368 | tf_op jit(solution)/shard_map/mul | solution.py:211
  5.7 33.3 %shard_map.91 = bf16[1296,128]{1,0:T(8,128)(2,1)} custom-call(bf16[1296,128]{1,0:T(8,128)(2,1)} %reshape.59.pair_ref, bf16[1296,128]{1,0:T(8,128)(2,1)} %reshape.60.pair_t_ref, f32[1296,1]{1,0:T(8,128)} %mul.62.mask_ref, f32[1296,1]{1,0:T(8,128)} %mul.63.mask_t_ref, f32[1,128]{1,0:T(1,128)} %bitcast.9, f32[1,128]{1,0:T(1,128)} %bitcast.10, ...), custom_call_target="tpu_custom_call" | custom-call | tf_op jit(solution)/shard_map/pallas_call | solution.py:218
  39.0 1.0 %reshape.61 = bf16[36,36,128]{2,1,0:T(8,128)(2,1)S(1)} reshape(bf16[1296,128]{1,0:T(8,128)(2,1)} %shard_map.91) | data formatting | bytes 663552 | tf_op jit(solution)/shard_map/reshape | solution.py:253
  40.0 0.8 %copy.17 = bf16[36,36,128]{2,0,1:T(8,128)(2,1)} copy(bf16[36,36,128]{2,1,0:T(8,128)(2,1)S(1)} %reshape.61) | data formatting | bytes 663552 | tf_op jit(solution)/shard_map/reshape | solution.py:253
Async XLA Ops:
  0.0 0.7 %copy-start.1 = (s32[144]{0:T(256)S(1)}, s32[144]{0:T(256)}, u32[]{:S(2)}) copy-start(s32[144]{0:T(256)} %param.10) | copy-start | bytes 1732
  0.8 1.9 %copy-start = (bf16[36,36,128]{2,1,0:T(8,128)(2,1)S(1)}, bf16[36,36,128]{2,1,0:T(8,128)(2,1)}, u32[]{:S(2)}) copy-start(bf16[36,36,128]{2,1,0:T(8,128)(2,1)} %param.9) | copy-start | bytes 995332

commit v2 on v1

--- a/solution.py
+++ b/solution.py
@@ -24,9 +24,9 @@
 
 def kernel(
     nrow, ncol, row_tok, col_tok, parts,
-    pair_ref, pair_t_ref, mask_ref, mask_t_ref, in_gain, in_bias, w_in, w_gate, out_gain, out_bias, w_out,
+    pair_ref, flags_ref, in_gain, in_bias, w_in, w_gate, out_gain, out_bias, w_out,
     out_ref,
-    blocks, left, gate, wide, stage, sums_out, sums_own, sums_in,
+    blocks, left, gate, flat, turned, wide, stage, sums_out, sums_own, sums_in,
     z_send, z_recv, p_send, p_recv,
 ):
     hidden = w_out.shape[0]
@@ -71,12 +71,33 @@
         )
 
     gain, bias = in_gain[...], in_bias[...]
+    tokens = flags_ref.shape[1]
+    flags = flags_ref[...].astype(jnp.float32)
+
+    def pair_mask(outer_start, inner_start, outer, inner):
+        place = lax.broadcasted_iota(jnp.int32, (outer * inner, 1), 0).astype(jnp.float32)
+        major = jnp.floor((place + 0.5) * (1.0 / inner))
+        minor = place - major * inner
+        token = lax.broadcasted_iota(jnp.int32, (1, tokens), 1)
+        from_major = (token - outer_start).astype(jnp.float32) == major
+        from_minor = (token - inner_start).astype(jnp.float32) == minor
+        chosen = jnp.where(from_major, flags, 0.0) + jnp.where(from_minor, flags, 0.0)
+        count = jnp.dot(
+            chosen.astype(jnp.bfloat16), jnp.ones((tokens, hidden), jnp.bfloat16),
+            preferred_element_type=jnp.float32,
+        )
+        return jnp.where(count > 1.5, 1.0, 0.0)
 
     for chunk in range(chunks):
         span = pl.ds(chunk * rows, rows)
-        normed = layer_norm(pair_ref[span, :].astype(jnp.float32), gain, bias).astype(jnp.bfloat16)
+        for j in range(chunk_j):
+            at = chunk * chunk_j + j
+            flat[at * col_tok : (at + 1) * col_tok, :] = pair_ref[at].astype(jnp.float32)
+        normed = layer_norm(flat[span, :], gain, bias).astype(jnp.bfloat16)
+        flat[span, :] = normed.astype(jnp.float32)
         proj = jnp.dot(normed, w_in[:, 2 * hidden :], preferred_element_type=jnp.float32)
-        right = sigmoid(proj[:, :hidden]) * proj[:, hidden:] * mask_ref[span, :]
+        right = sigmoid(proj[:, :hidden]) * proj[:, hidden:]
+        right *= pair_mask(row * row_tok + chunk * chunk_j, col * col_tok, chunk_j, col_tok)
         blocks[row, chunk] = right.astype(jnp.bfloat16)
         if chunk == 0:
             neighbours = has_up.astype(jnp.int32) + has_down.astype(jnp.int32)
@@ -93,9 +114,14 @@
     k_step = col_tok // parts
     for part in range(parts):
         span = pl.ds(part * sum_rows, sum_rows)
-        normed = layer_norm(pair_t_ref[span, :].astype(jnp.float32), gain, bias).astype(jnp.bfloat16)
+        for k in range(k_step):
+            turned[k * row_tok : (k + 1) * row_tok, :] = flat[
+                pl.ds(part * k_step + k, row_tok, stride=col_tok), :
+            ]
+        normed = turned[...].astype(jnp.bfloat16)
         proj = jnp.dot(normed, w_in[:, : 2 * hidden], preferred_element_type=jnp.float32)
-        value = sigmoid(proj[:, :hidden]) * proj[:, hidden:] * mask_t_ref[span, :]
+        value = sigmoid(proj[:, :hidden]) * proj[:, hidden:]
+        value *= pair_mask(col * col_tok + part * k_step, row * row_tok, k_step, row_tok)
         value = value.astype(jnp.bfloat16).astype(jnp.float32)
         for k in range(k_step):
             left[part * k_step + k, :row_tok, :] = value[k * row_tok : (k + 1) * row_tok]
@@ -177,7 +203,10 @@
         normed = layer_norm(total, out_gain[...], out_bias[...]).astype(jnp.bfloat16)
         projected = jnp.dot(normed, w_out[...], preferred_element_type=jnp.float32)
         span = pl.ds(part * sum_rows, sum_rows)
-        out_ref[span, :] = (gate[span, :] * projected).astype(jnp.bfloat16)
+        flat[span, :] = gate[span, :] * projected
+
+    for i in range(row_tok):
+        out_ref[i] = flat[pl.ds(i, col_tok, stride=row_tok), :].astype(jnp.bfloat16)
 
     def drain_rows(index, carry):
         block, chunk = index // chunks, lax.rem(index, chunks)
@@ -203,13 +232,7 @@
     row_tok, col_tok, channels = pair.shape
     hidden = w_out.shape[0]
     parts = 3
-    row_start = lax.axis_index("row") * row_tok
-    col_start = lax.axis_index("col") * col_tok
-    row_flags = lax.dynamic_slice_in_dim(token_mask, row_start, row_tok, 0).astype(jnp.float32)
-    col_flags = lax.dynamic_slice_in_dim(token_mask, col_start, col_tok, 0).astype(jnp.float32)
     total = row_tok * col_tok
-    mask = (row_flags[:, None] * col_flags[None, :]).reshape(total, 1)
-    mask_t = (col_flags[:, None] * row_flags[None, :]).reshape(total, 1)
     chunks = row_tok // col_tok * parts
     rows = col_tok // parts * col_tok
     sum_rows = col_tok // parts * row_tok
@@ -217,13 +240,15 @@
     vmem = pl.BlockSpec(memory_space=pltpu.VMEM)
     result = pl.pallas_call(
         functools.partial(kernel, nrow, ncol, row_tok, col_tok, parts),
-        out_shape=jax.ShapeDtypeStruct((total, channels), jnp.bfloat16),
-        in_specs=[vmem] * 11,
+        out_shape=jax.ShapeDtypeStruct(pair.shape, jnp.bfloat16),
+        in_specs=[vmem] * 9,
         out_specs=vmem,
         scratch_shapes=[
             pltpu.VMEM((nrow, chunks, rows, hidden), jnp.bfloat16),
             pltpu.VMEM((col_tok, padded, hidden), jnp.float32),
             pltpu.VMEM((total, channels), jnp.float32),
+            pltpu.VMEM((total, channels), jnp.float32),
+            pltpu.VMEM((sum_rows, channels), jnp.float32),
             pltpu.VMEM((rows, hidden), jnp.float32),
             pltpu.VMEM((JTILE * row_tok, hidden), jnp.float32),
             pltpu.VMEM((ncol, parts, sum_rows, hidden), jnp.bfloat16),
@@ -238,10 +263,8 @@
             collective_id=0, has_side_effects=True, vmem_limit_bytes=56 * 1024 * 1024
         ),
     )(
-        pair.reshape(total, channels),
-        pair.transpose(1, 0, 2).reshape(total, channels),
-        mask,
-        mask_t,
+        pair,
+        token_mask[None, :],
         in_gain[None, :],
         in_bias[None, :],
         w_in,
@@ -250,7 +273,7 @@
         out_bias[None, :],
         w_out,
     )
-    return result.reshape(col_tok, row_tok, channels).transpose(1, 0, 2)
+    return result
 
 
 def solution(mesh):

time: 41.3 us -> 35.1 us (0.85)
  local copies, waits for them, and re-layouts: 7.35 us -> 1.76 us
  Pallas kernels: 33.3 us -> 32.8 us
    reshape x4 -> x0, local copies, waits for them, and re-layouts: 4.44 us -> none  [the longest x2 1.83 us: local(): return result.reshape(col_tok, row_tok, channels).transpose(1, 0, 2)]
    mul x2 -> x0, local copies, waits for them, and re-layouts: 2.18 us -> none  [the longest x1 1.09 us: local(): mask = (row_flags[:, None] * col_flags[None, :]).reshape(total, 1)]
    unnamed x4 -> x1, local copies, waits for them, and re-layouts: 0.68 us -> 1.76 us
    pallas_call x1, Pallas kernels: 33.3 us -> 32.8 us  [local(): pl.pallas_call(functools.partial(kernel, nrow, ncol, row_tok, col_tok, pa...]
where the time goes in v2:
time: 35.1 us; the launch traced here: 34.6 us
  Pallas kernels  32.8 us (93%)
  local copies, waits for them, and re-layouts  1.76 us (5%)
    pallas_call x1, Pallas kernels, local(): pl.pallas_call(functools.partial(kernel, nrow, ncol, row_tok, col_tok, pa...  32.8 us
    unnamed x1, local copies, waits for them, and re-layouts  1.76 us

profile of v2, /device:TPU:0, one launch (start us, length us, event | category | flops | bytes accessed | tf_op | source)
XLA Modules:
  0.0 34.6 jit_solution(8813074261507176314)
XLA Ops:
  0.0 32.8 %shard_map.91 = bf16[36,36,128]{2,1,0:T(8,128)(2,1)} custom-call(bf16[36,36,128]{2,1,0:T(8,128)(2,1)} %pair_ref.1, s32[1,144]{1,0:T(1,128)} %bitcast.5, f32[1,128]{1,0:T(1,128)} %bitcast.6, f32[1,128]{1,0:T(1,128)} %bitcast.7, bf16[128,512]{1,0:T(8,128)(2,1)} %w_in.1, bf16[128,128]{1,0:T(8,128)(2,1)} %w_gate.1, f32[1,128]{1,0:T(1,128)} %bitcast.8, ...), custom_call_target="tpu_custom_call" | custom-call | tf_op jit(solution)/shard_map/pallas_call | solution.py:241
  32.8 1.8 %copy.11 = bf16[36,36,128]{2,1,0:T(8,128)(2,1)} copy(bf16[36,36,128]{2,1,0:T(8,128)(2,1)} %shard_map.91) | data formatting | bytes 663552

commit v3 on v2

--- a/solution.py
+++ b/solution.py
@@ -24,12 +24,30 @@
 
 def kernel(
     nrow, ncol, row_tok, col_tok, parts,
-    pair_ref, flags_ref, in_gain, in_bias, w_in, w_gate, out_gain, out_bias, w_out,
-    out_ref,
-    blocks, left, gate, flat, turned, wide, stage, sums_out, sums_own, sums_in,
-    z_send, z_recv, p_send, p_recv,
+    *refs,
 ):
+    pair_hbm, hbm_refs, out_ref = refs[0], refs[1:9], refs[9]
+    pair_ref, near_refs, pair_sem, near_sem = refs[10], refs[11:19], refs[19], refs[20]
+    flags_ref, in_gain, in_bias, w_in, w_gate, out_gain, out_bias, w_out = near_refs
+    (
+        blocks, left, gate, flat, turned, wide, stage, sums_out, sums_own, sums_in, z_send, z_recv, p_send, p_recv,
+    ) = refs[21:]
     hidden = w_out.shape[0]
+
+    def fetch_pair(chunk):
+        span = pl.ds(chunk * (col_tok // parts), col_tok // parts)
+        return pltpu.make_async_copy(pair_hbm.at[span], pair_ref.at[span], pair_sem.at[chunk])
+
+    def fetch(index):
+        return pltpu.make_async_copy(hbm_refs[index], near_refs[index], near_sem.at[index])
+
+    fetch_pair(0).start()
+    for index in range(4):
+        fetch(index).start()
+    for chunk in range(1, row_tok // col_tok * parts):
+        fetch_pair(chunk).start()
+    for index in range(4, 8):
+        fetch(index).start()
     group, row, col = lax.axis_index("groups"), lax.axis_index("row"), lax.axis_index("col")
     per_row = row_tok // col_tok
     chunks = per_row * parts
@@ -70,6 +88,8 @@
             p_send.at[target, part], p_recv.at[source, part], (group, row, target), MESH,
         )
 
+    for index in range(4):
+        fetch(index).wait()
     gain, bias = in_gain[...], in_bias[...]
     tokens = flags_ref.shape[1]
     flags = flags_ref[...].astype(jnp.float32)
@@ -90,6 +110,7 @@
 
     for chunk in range(chunks):
         span = pl.ds(chunk * rows, rows)
+        fetch_pair(chunk).wait()
         for j in range(chunk_j):
             at = chunk * chunk_j + j
             flat[at * col_tok : (at + 1) * col_tok, :] = pair_ref[at].astype(jnp.float32)
@@ -110,6 +131,9 @@
         @pl.when(has_down)
         def _():
             down_copy(row, chunk).start()
+
+    for index in range(4, 8):
+        fetch(index).wait()
 
     k_step = col_tok // parts
     for part in range(parts):
@@ -237,42 +261,37 @@
     rows = col_tok // parts * col_tok
     sum_rows = col_tok // parts * row_tok
     padded = -(-row_tok // 8) * 8
-    vmem = pl.BlockSpec(memory_space=pltpu.VMEM)
+    operands = [pair, token_mask[None, :], in_gain[None, :], in_bias[None, :], w_in, w_gate]
+    operands += [out_gain[None, :], out_bias[None, :], w_out]
+    scratch = [pltpu.VMEM(operand.shape, operand.dtype) for operand in operands]
+    scratch += [
+        pltpu.SemaphoreType.DMA((chunks,)),
+        pltpu.SemaphoreType.DMA((8,)),
+        pltpu.VMEM((nrow, chunks, rows, hidden), jnp.bfloat16),
+        pltpu.VMEM((col_tok, padded, hidden), jnp.float32),
+        pltpu.VMEM((total, channels), jnp.float32),
+        pltpu.VMEM((total, channels), jnp.float32),
+        pltpu.VMEM((sum_rows, channels), jnp.float32),
+        pltpu.VMEM((rows, hidden), jnp.float32),
+        pltpu.VMEM((JTILE * row_tok, hidden), jnp.float32),
+        pltpu.VMEM((ncol, parts, sum_rows, hidden), jnp.bfloat16),
+        pltpu.VMEM((parts, sum_rows, hidden), jnp.float32),
+        pltpu.VMEM((ncol, parts, sum_rows, hidden), jnp.bfloat16),
+        pltpu.SemaphoreType.DMA((2, nrow, chunks)),
+        pltpu.SemaphoreType.DMA((nrow, chunks)),
+        pltpu.SemaphoreType.DMA((ncol, parts)),
+        pltpu.SemaphoreType.DMA((ncol, parts)),
+    ]
     result = pl.pallas_call(
         functools.partial(kernel, nrow, ncol, row_tok, col_tok, parts),
         out_shape=jax.ShapeDtypeStruct(pair.shape, jnp.bfloat16),
-        in_specs=[vmem] * 9,
-        out_specs=vmem,
-        scratch_shapes=[
-            pltpu.VMEM((nrow, chunks, rows, hidden), jnp.bfloat16),
-            pltpu.VMEM((col_tok, padded, hidden), jnp.float32),
-            pltpu.VMEM((total, channels), jnp.float32),
-            pltpu.VMEM((total, channels), jnp.float32),
-            pltpu.VMEM((sum_rows, channels), jnp.float32),
-            pltpu.VMEM((rows, hidden), jnp.float32),
-            pltpu.VMEM((JTILE * row_tok, hidden), jnp.float32),
-            pltpu.VMEM((ncol, parts, sum_rows, hidden), jnp.bfloat16),
-            pltpu.VMEM((parts, sum_rows, hidden), jnp.float32),
-            pltpu.VMEM((ncol, parts, sum_rows, hidden), jnp.bfloat16),
-            pltpu.SemaphoreType.DMA((2, nrow, chunks)),
-            pltpu.SemaphoreType.DMA((nrow, chunks)),
-            pltpu.SemaphoreType.DMA((ncol, parts)),
-            pltpu.SemaphoreType.DMA((ncol, parts)),
-        ],
+        in_specs=[pl.BlockSpec(memory_space=pltpu.HBM)] * 9,
+        out_specs=pl.BlockSpec(memory_space=pltpu.VMEM),
+        scratch_shapes=scratch,
         compiler_params=pltpu.CompilerParams(
             collective_id=0, has_side_effects=True, vmem_limit_bytes=56 * 1024 * 1024
         ),
-    )(
-        pair,
-        token_mask[None, :],
-        in_gain[None, :],
-        in_bias[None, :],
-        w_in,
-        w_gate,
-        out_gain[None, :],
-        out_bias[None, :],
-        w_out,
-    )
+    )(*operands)
     return result
 
 

time: 35.1 us -> 34.1 us (0.972)
  Pallas kernels: 32.8 us -> 31.8 us
    pallas_call x1, Pallas kernels: 32.8 us -> 31.8 us  [local(): pl.pallas_call(functools.partial(kernel, nrow, ncol, row_tok, col_tok, pa...]
where the time goes in v3:
time: 34.1 us; the launch traced here: 33.6 us
  Pallas kernels  31.8 us (93%)
  local copies, waits for them, and re-layouts  1.76 us (5%)
    pallas_call x1, Pallas kernels, local(): pl.pallas_call(functools.partial(kernel, nrow, ncol, row_tok, col_tok, pa...  31.8 us
    unnamed x1, local copies, waits for them, and re-layouts  1.76 us

profile of v3, /device:TPU:0, one launch (start us, length us, event | category | flops | bytes accessed | tf_op | source)
XLA Modules:
  0.0 33.6 jit_solution(6542915191512501433)
XLA Ops:
  0.0 31.8 %shard_map.91 = bf16[36,36,128]{2,1,0:T(8,128)(2,1)} custom-call(bf16[36,36,128]{2,1,0:T(8,128)(2,1)} %refs_0_.1, s32[1,144]{1,0:T(1,128)} %bitcast.5, f32[1,128]{1,0:T(1,128)} %bitcast.6, f32[1,128]{1,0:T(1,128)} %bitcast.7, bf16[128,512]{1,0:T(8,128)(2,1)} %refs_4_.1, bf16[128,128]{1,0:T(8,128)(2,1)} %refs_5_.1, f32[1,128]{1,0:T(1,128)} %bitcast.8, ...), custom_call_target="tpu_custom_call" | custom-call | tf_op jit(solution)/shard_map/pallas_call | solution.py:285
  31.8 1.8 %copy.11 = bf16[36,36,128]{2,1,0:T(8,128)(2,1)} copy(bf16[36,36,128]{2,1,0:T(8,128)(2,1)} %shard_map.91) | data formatting | bytes 663552
